TPU v7x, 128 devices: a whole 4x4x4 slice. The times are simulated.
128 devices in a mesh: dp: 16 (over y, z_lo, core), mp: 8 (over x, z_hi).
Axes of the slice: x: 4, y: 4, z: 4 (z_hi: 2, z_lo: 2; z = z_hi * 2 + z_lo), core: 2. Of those that a mesh axis runs over, the one named last changes fastest.
Arguments:
- layer_input: bfloat16 [16384, 8192], P(('dp', 'mp'))
- norm_gain: float32 [8192], replicated, may hold values from 0.5 to 1.5
- query_weight: bfloat16 [8192, 4096], P(None, 'mp'), may hold values from -0.0625 to 0.0625
- key_weight: bfloat16 [8192, 1024], P(None, 'mp'), may hold values from -0.0625 to 0.0625
- value_weight: bfloat16 [8192, 1024], P(None, 'mp'), may hold values from -0.0625 to 0.0625
- query_grad: bfloat16 [16384, 4096], P('dp', 'mp'), may hold values from -12 to 12
- key_grad: bfloat16 [16384, 1024], P('dp', 'mp'), may hold values from -12 to 12
- value_grad: bfloat16 [16384, 1024], P('dp', 'mp'), may hold values from -12 to 12
- positions: int32 [16384], P('dp'), may hold values from 0 to 1022, as said below
Outputs:
- input_grad: bfloat16 [16384, 8192], P(('dp', 'mp'))
- key_weight_grad: float32 [8192, 1024], P('dp', 'mp')
- value_weight_grad: float32 [8192, 1024], P('dp', 'mp')
- query_weight_grad: float32 [8192, 4096], P('dp', 'mp')
Inputs may be any that keep to these rules, and one draw needn't show every extreme that they name: Each slab of 1024 consecutive tokens holds a prompt at positions 0 upward, then a first completion continuing from the prompt's end, then a second completion that restarts at the prompt's end.
All inputs are finite; a program needn't handle non-finite values.
Results may differ from a plain program's by a relative error of at most 0.023.
Values may be sent and summed in bfloat16 or wider, within the bound.
A program may use at most 192 MiB of HBM per device.

v0:
```python
import math

import jax
import jax.numpy as jnp
from jax import lax
from jax.sharding import PartitionSpec as P

HD = 128


def normalize(rows, norm_gain):
    value_rows = rows.astype(jnp.float32)
    inverse_deviation = lax.rsqrt(jnp.mean(value_rows * value_rows, axis=-1, keepdims=True) + 1e-05)
    normed = (value_rows * inverse_deviation * norm_gain).astype(jnp.bfloat16)
    return (normed, inverse_deviation)


def rope_back(grad, positions, head_size):
    count, width = grad.shape
    half = head_size // 2
    value_rows = grad.astype(jnp.float32).reshape(count, width // head_size, head_size)
    index = jnp.arange(half, dtype=jnp.float32)
    freq = jnp.exp(-(2.0 * index / head_size) * jnp.log(10000.0))
    angle = positions.astype(jnp.float32)[:, None] * freq[None, :]
    cosine = jnp.cos(angle)[:, None, :]
    sine = jnp.sin(angle)[:, None, :]
    first = value_rows[..., :half]
    second = value_rows[..., half:]
    back = jnp.concatenate(
        [first * cosine + second * sine, second * cosine - first * sine], axis=-1
    )
    return back.reshape(count, width).astype(jnp.bfloat16)


def shards(
    layer_input,
    norm_gain,
    query_weight,
    key_weight,
    value_weight,
    query_grad,
    key_grad,
    value_grad,
    positions,
):
    cols = key_weight.shape[1]
    qcols = query_weight.shape[1]
    total_tokens = key_grad.shape[0] * lax.axis_size("dp")
    key_backward_grad = rope_back(key_grad, positions, HD)
    query_back = rope_back(query_grad, positions, HD)
    cotangent = jnp.concatenate([query_back, key_backward_grad, value_grad], axis=1)
    weights = jnp.concatenate([query_weight, key_weight, value_weight], axis=1)
    normed_own, inverse_deviation = normalize(layer_input, norm_gain)
    normed_piece, unused_rstd = normalize(
        lax.all_gather(layer_input, "mp", axis=0, tiled=True), norm_gain
    )
    partial_grads = lax.dot_general(
        normed_piece, cotangent, (((0,), (0,)), ((), ())), preferred_element_type=jnp.float32
    )
    normed_grad = lax.psum_scatter(
        lax.dot_general(
            cotangent, weights, (((1,), (1,)), ((), ())), preferred_element_type=jnp.float32
        ).astype(jnp.bfloat16),
        "mp",
        scatter_dimension=0,
        tiled=True,
    ).astype(jnp.float32)
    summed_grads = lax.psum_scatter(
        partial_grads.astype(jnp.bfloat16), "dp", scatter_dimension=0, tiled=True
    ).astype(jnp.float32)
    factor = 1.0 / math.sqrt(total_tokens)
    summed_grads = summed_grads * factor
    value_rows = layer_input.astype(jnp.float32)
    gain_scaled_rows = normed_grad * norm_gain
    centered_input_unit = value_rows * inverse_deviation
    backward_result = inverse_deviation * (
        gain_scaled_rows
        - centered_input_unit
        * jnp.mean(centered_input_unit * gain_scaled_rows, axis=-1, keepdims=True)
    )
    query_part = summed_grads[:, :qcols]
    key_part = summed_grads[:, qcols : qcols + cols]
    value_part = summed_grads[:, qcols + cols :]
    return (backward_result.astype(jnp.bfloat16), key_part, value_part, query_part)


def solution(mesh):
    in_specs = (
        P(("dp", "mp"), None),
        P(),
        P(None, "mp"),
        P(None, "mp"),
        P(None, "mp"),
        P("dp", "mp"),
        P("dp", "mp"),
        P("dp", "mp"),
        P("dp"),
    )
    out_specs = (P(("dp", "mp"), None), P("dp", "mp"), P("dp", "mp"), P("dp", "mp"))
    return jax.shard_map(shards, mesh=mesh, in_specs=in_specs, out_specs=out_specs, check_vma=False)
```

profile of v0, /device:TPU:1, one launch (start us, length us, event | category | flops | bytes accessed | tf_op | source)
XLA Modules:
  0.0 544.5 jit_solution(9979788778329375626)
XLA Ops:
  7.2 0.0 copy-start.2
  7.2 0.0 all-gather.2.cloned.1.call-start
  7.2 0.7 all-gather.2.cloned.1.call-update
  7.9 0.0 reduce-scatter.3.cloned.1.call-start
  8.0 0.7 convert_element_type.40
  8.6 1.1 copy.13
  9.8 1.2 fusion.27
  11.0 0.2 copy.14
  11.2 0.0 copy-done.2
  11.2 0.7 reshape.148
  11.9 1.9 multiply_cosine_fusion
  13.8 1.8 add_convert_fusion
  15.6 0.0 copy-start.4
  15.6 1.4 pad_maximum_fusion.1
  17.0 0.2 copy.17
  17.2 0.0 copy-done.4
  17.2 19.2 %convolution_convert_fusion = bf16[1024,8192]{1,0:T(8,128)(2,1)} fusion(bf16[8192,128]{1,0:T(8,128)(2,1)S(1)} %copy-done.4, bf16[8192,128]{1,0:T(8,128)(2,1)} %param.12, bf16[8192,512]{1,0:T(8,128)(2,1)} %param.11, bf16[1024,128]{1,0:T(8,128)(2,1)} %param.16, bf16[1024,128]{1,0:T(8,128)(2,1)S(1)} %copy.14, bf16[1024,512]{1,0:T(8,128)(2,1)S(1)} %bitcast.10), kind=kOutput, calls=%fused_computation.8 | convolution fusion | flops 12935757824 | bytes 30932992 | tf_op jit(solution)/shard_map/dot_general | solution.py:61
  36.4 0.0 reduce-scatter.3.cloned.1.call-update
  36.4 0.0 copy-start.3
  36.5 0.0 copy-start.5
  36.5 0.2 reduce-scatter.5.cloned.1.call-start
  36.7 162.5 %all-gather.2.cloned.1.call-done = bf16[1024,8192]{1,0:T(8,128)(2,1)} async-done(((bf16[128,8192]{1,0:T(8,128)(2,1)}), bf16[1024,8192]{1,0:T(8,128)(2,1)}) %all-gather.2.cloned.1.call-update) | async-done | bytes 16777232 | tf_op jit(solution)/shard_map/all_gather | solution.py:55
  199.2 7.2 %fusion = f32[1024]{0:T(1024)S(1)} fusion(bf16[1024,8192]{1,0:T(8,128)(2,1)} %all-gather.2.cloned.1.call-done), kind=kLoop, calls=%fused_computation.2 | loop fusion | flops 25164800 | bytes 16781312 | tf_op jit(solution)/shard_map/reduce_sum | solution.py:13
  206.4 0.0 copy-done.3
  206.4 0.0 copy-done.5
  206.4 29.3 %fusion.7 = bf16[8192,768]{1,0:T(8,128)(2,1)} fusion(bf16[1024,8192]{1,0:T(8,128)(2,1)} %all-gather.2.cloned.1.call-done, f32[8192]{0:T(1024)S(1)} %copy-done.3, f32[1024]{0:T(1024)S(1)} %add_rsqrt_fusion, bf16[1024,128]{1,0:T(8,128)(2,1)S(1)} %copy-done.5, bf16[1024,128]{1,0:T(8,128)(2,1)S(1)} %copy.14, bf16[1024,512]{1,0:T(8,128)(2,1)S(1)} %bitcast.11), kind=kOutput, calls=%fused_computation.9 | convolution fusion | flops 12929466368 | bytes 30969856 | tf_op jit(solution)/shard_map/dot_general | solution.py:57
  235.7 0.0 copy-start
  235.7 0.0 reduce-scatter.5.cloned.1.call-update
  235.7 1.6 copy-done
  237.4 0.5 fusion.21
  237.9 153.8 %reduce-scatter.3.cloned.1.call-done = bf16[128,8192]{1,0:T(8,128)(2,1)} async-done(((bf16[1024,8192]{1,0:T(8,128)(2,1)}), bf16[128,8192]{1,0:T(8,128)(2,1)}) %reduce-scatter.3.cloned.1.call-update) | async-done | bytes 2097168 | tf_op jit(solution)/shard_map/reduce_scatter | solution.py:60
  391.6 0.0 copy-start.1
  391.6 2.7 fusion.17
  394.3 0.0 copy-done.1
  394.3 2.4 fusion.20
  396.7 138.1 %reduce-scatter.5.cloned.1.call-done = bf16[512,768]{1,0:T(8,128)(2,1)} async-done(((bf16[8192,768]{1,0:T(8,128)(2,1)}), bf16[512,768]{1,0:T(8,128)(2,1)}) %reduce-scatter.5.cloned.1.call-update) | async-done | bytes 786448 | tf_op jit(solution)/shard_map/reduce_scatter | solution.py:68
  534.8 1.2 convert_multiply_fusion.5
  536.0 0.8 fusion.32
  536.9 1.1 slice.34
  (6 shorter events, 0.1 us)
Async XLA Ops:
  7.2 4.0 copy-start.2
  7.2 192.0 %all-gather.2.cloned.1.call-start = ((), (), s32[]{:S(2)}) async-start(), calls=%async_computation.3 | async-start | bytes 18874368 | tf_op jit(solution)/shard_map/all_gather | solution.py:55
  7.9 383.7 %reduce-scatter.3.cloned.1.call-start = ((), (), s32[]{:S(2)}) async-start(), calls=%async_computation.2 | async-start | bytes 18874368 | tf_op jit(solution)/shard_map/reduce_scatter | solution.py:60
  15.6 1.6 copy-start.4
  36.4 169.9 %copy-start.3 = (f32[8192]{0:T(1024)S(1)}, f32[8192]{0:T(1024)}, u32[]{:S(2)}) copy-start(f32[8192]{0:T(1024)} %param.10) | copy-start | bytes 98308
  36.5 169.9 %copy-start.5 = (bf16[1024,128]{1,0:T(8,128)(2,1)S(1)}, bf16[1024,128]{1,0:T(8,128)(2,1)}, u32[]{:S(2)}) copy-start(bf16[1024,128]{1,0:T(8,128)(2,1)} %param.16) | copy-start | bytes 786436
  36.5 498.3 %reduce-scatter.5.cloned.1.call-start = ((), (), s32[]{:S(2)}) async-start(), calls=%async_computation.4 | async-start | bytes 13369344 | tf_op jit(solution)/shard_map/reduce_scatter | solution.py:68
  235.7 1.6 copy-start
  391.6 2.7 copy-start.1
Sparse Core Ops, SparseCore 0:
  10.3 188.7 all-gather.1
  203.1 188.4 reduce-scatter.2
  394.0 140.7 reduce-scatter.4
where the time goes:
time: 545 us
  waiting for transfers between devices  455 us (83%)
  matrix products  48.5 us (9%)
  other arithmetic  21.1 us (4%)
  between operations  13.9 us (3%)
  local copies, waits for them, and re-layouts  5.73 us (1%)
    all_gather x1, waiting for transfers between devices, shards(): lax.all_gather(layer_input, 'mp', axis=0, tiled=True)  162 us
    reduce_scatter x1, waiting for transfers between devices, shards(): lax.psum_scatter(lax.dot_general(cotangent, weights, (((1,), (1,)), ((),...  154 us
    reduce_scatter x1, waiting for transfers between devices, shards(): lax.psum_scatter(partial_grads.astype(jnp.bfloat16), 'dp', scatter_dimens...  138 us
    dot_general x1, matrix products, shards(): lax.dot_general(normed_piece, cotangent, (((0,), (0,)), ((), ())), prefer...  29.3 us
    dot_general x1, matrix products, shards(): lax.dot_general(cotangent, weights, (((1,), (1,)), ((), ())), preferred_e...  19.2 us
  transfers between devices with their start and end apart: 3, of which 3 were waited for; matrix products, arithmetic and copies ran while one was open for 13% of the time, Pallas kernels for 0%

commit v1 on v0

v1 whole, which is shorter than its diff:
```python
import functools
import math

import jax
import jax.numpy as jnp
from jax import lax
from jax.experimental import pallas as pl
from jax.experimental.pallas import tpu as pltpu
from jax.sharding import PartitionSpec as P

HD = 128
NY, NX = 4, 4
HOPS = (1, 3, 2)
BF = jnp.bfloat16
F32 = jnp.float32
MESH = pl.DeviceIdType.MESH


def mult(value, by):
    return pl.multiple_of(value, by)


def core_kernel(
    x_ref, gain_ref, wq_ref, wk_ref, wv_ref, q_ref, k_ref, v_ref, pos_ref, freq_ref,
    dxs_ref, dws_ref,
    nt, xst, cot, wb, coresend, corerecv, sum2, yrecv, zlsend, zlrecv, xsend, dxsend, dxrecv, dxown,
    w_s, w_r, wl_s, wy_s, wy_r, wc_s, wc_r, x_s, x_r, xl_s, xz_s, xz_r, c_s, c_r,
    pc_s, pc_r, py_s, py_r, pz_s, pz_r, px_s, px_r, pl_s, dz_s, dz_r, da_s, da_r, dl_s,
):
    dp = lax.axis_index("dp")
    mp = lax.axis_index("mp")
    y, zl, core = dp // 4, (dp // 2) % 2, dp % 2
    x, zh = mp // 2, mp % 2

    def at(y=y, zl=zl, core=core, x=x, zh=zh):
        return (y * 4 + zl * 2 + core, x * 2 + zh)

    def hop(v, k):
        return lax.rem(v + k, 4)

    def remote(src, dst, ssem, rsem, where):
        return pltpu.make_async_remote_copy(
            src_ref=src, dst_ref=dst, send_sem=ssem, recv_sem=rsem,
            device_id=where, device_id_type=MESH,
        )

    peers = [at(x=hop(x, k)) for k in HOPS] + [at(y=hop(y, k)) for k in HOPS]
    peers += [at(zl=1 - zl), at(zh=1 - zh), at(core=1 - core)]
    barrier = pltpu.get_barrier_semaphore()
    for peer in peers:
        pl.semaphore_signal(barrier, inc=1, device_id=peer, device_id_type=MESH)
    pl.semaphore_wait(barrier, len(peers))

    own_rows = core * 8 + y * 2
    widths = ((wq_ref, 0, 512), (wk_ref, 512, 128), (wv_ref, 640, 128))

    def w_part(j, to_x):
        ref, low, width = widths[j]
        src = ref.at[y, :, core, to_x]
        dst = wb.at[pl.ds(own_rows, 2), :, pl.ds(mult(x * 768 + low, 128), width)]
        return src, dst

    w_copies = []
    for i, k in enumerate(HOPS):
        for j in range(3):
            src, dst = w_part(j, hop(x, k))
            copy = remote(src, dst, w_s.at[i, j], w_r.at[i, j], at(x=hop(x, k)))
            copy.start()
            w_copies.append(copy)
    w_local = []
    for j in range(3):
        src, dst = w_part(j, x)
        copy = pltpu.make_async_copy(src, dst, wl_s.at[j])
        copy.start()
        w_local.append(copy)

    def squares(c, total):
        piece = x_ref[:, pl.ds(mult(c * 512, 512), 512)].astype(F32)
        piece = piece * piece
        return total + (piece[:, :128] + piece[:, 128:256]) + (piece[:, 256:384] + piece[:, 384:])

    total = lax.fori_loop(0, 16, squares, jnp.zeros((128, 128), F32))
    mean = jnp.sum(total, axis=1, keepdims=True) * (1.0 / 8192)
    rstd = lax.rsqrt(mean + 1e-05)

    def x_to(to_x):
        def block(kappa, carry):
            c, yy, zz = kappa // 8, (kappa // 2) % 4, kappa % 2
            low = mult((yy * 4 + zz * 2 + c) * 512 + to_x * 128, 128)
            rows = x_ref[:, pl.ds(low, 128)].astype(F32)
            normed = rows * rstd * gain_ref[:, pl.ds(low, 128)]
            nt[to_x, kappa] = normed.T.astype(BF)
            return carry

        lax.fori_loop(0, 16, block, 0)

    x_slot = pl.ds(mult((zh * 4 + x) * 128, 128), 128)
    x_copies = []
    for i, k in enumerate(HOPS):
        to_x = hop(x, k)
        x_to(to_x)
        copy = remote(nt.at[to_x], xst.at[:, :, x_slot], x_s.at[i], x_r.at[i], at(x=to_x))
        copy.start()
        x_copies.append(copy)
    x_to(x)
    x_local = pltpu.make_async_copy(nt.at[x], xst.at[:, :, x_slot], xl_s)
    x_local.start()

    def x_forward(i, from_x):
        slot = pl.ds(mult((zh * 4 + from_x) * 128, 128), 128)
        copy = remote(xst.at[:, :, slot], xst.at[:, :, slot], xz_s.at[i], xz_r.at[i], at(zh=1 - zh))
        copy.start()
        return copy

    x_local.wait()
    xz_copies = [x_forward(3, x)]

    lane = lax.broadcasted_iota(jnp.int32, (128, 128), 1)

    def rope(t, carry):
        block = (t % 4) * 2 + t // 4
        rows = pl.ds(mult(block * 128, 128), 128)
        place = jnp.broadcast_to(pos_ref[pl.ds(block, 1), :].astype(F32), (128, 128)).T
        angle = place * freq_ref[...]
        cosine = jnp.cos(angle)
        sine = jnp.sin(angle)
        sine = jnp.where(lane < 64, sine, -sine)
        out = pl.ds(mult(t * 128, 128), 128)
        for h in range(5):
            v = q_ref[rows, pl.ds(h * 128, 128)] if h < 4 else k_ref[rows, :]
            v = v.astype(F32)
            back = v * cosine + pltpu.roll(v, 64, 1) * sine
            cot[out, pl.ds(mult(x * 768 + h * 128, 128), 128)] = back.astype(BF)
        cot[out, pl.ds(mult(x * 768 + 640, 128), 128)] = v_ref[rows, :]
        return carry

    lax.fori_loop(0, 8, rope, 0)

    for copy in w_local:
        copy.wait()
    for copy in w_copies:
        copy.wait_recv()
    mine = wb.at[pl.ds(own_rows, 2)]
    wy_copies = []
    for i, k in enumerate(HOPS):
        copy = remote(mine, mine, wy_s.at[i], wy_r.at[i], at(y=hop(y, k)))
        copy.start()
        wy_copies.append(copy)

    def w_core(i, from_y):
        rows = wb.at[pl.ds(core * 8 + from_y * 2, 2)]
        copy = remote(rows, rows, wc_s.at[i], wc_r.at[i], at(core=1 - core))
        copy.start()
        return copy

    wc_copies = [w_core(3, y)]
    for i, k in enumerate(HOPS):
        x_copies[i].wait_recv()
        xz_copies.append(x_forward(i, hop(x, 4 - k)))

    def cot_copy(i, row, rows):
        part = cot.at[pl.ds(mult(row, 512), rows), pl.ds(mult(x * 768, 128), 768)]
        return part

    c_copies = []
    for i in range(2):
        part = cot_copy(i, 0, 1024)
        copy = remote(part, part, c_s.at[i], c_r.at[i], at(x=hop(x, HOPS[i])))
        copy.start()
        c_copies.append(copy)

    for i, k in enumerate(HOPS):
        wy_copies[i].wait_recv()
        wc_copies.append(w_core(i, hop(y, 4 - k)))
    for copy in xz_copies:
        copy.wait_recv()

    blocks = (x, hop(x, 3), hop(x, 1), hop(x, 2))

    def wdot(kappa, b):
        return jnp.dot(
            xst[pl.ds(kappa, 2)].reshape(256, 1024),
            cot[:, pl.ds(mult(b * 768, 128), 768)],
            preferred_element_type=F32,
        )

    def pc_copy(r, k):
        return remote(coresend.at[r % 2, k], corerecv.at[r, k], pc_s.at[r, k], pc_r.at[r, k], at(core=1 - core))

    def py_copy(r, k):
        return remote(sum2.at[r, k], yrecv.at[r, k], py_s.at[r, k], py_r.at[r, k], at(y=hop(y, 1 + k)))

    def pz_copy(r):
        return remote(zlsend.at[r], zlrecv.at[r], pz_s.at[r], pz_r.at[r], at(zl=1 - zl))

    def px_copy(r):
        if r == 0:
            return pltpu.make_async_copy(xsend.at[r], dws_ref.at[x], pl_s)
        return remote(xsend.at[r], dws_ref.at[x], px_s.at[r - 1], px_r.at[r - 1], at(x=blocks[r]))

    def wgrad(r):
        b = blocks[r]

        def other(k, carry):
            if r >= 2:
                pc_copy(r - 2, k).wait_send()
            coresend[r % 2, k] = wdot((1 - core) * 8 + hop(y, 1 + k) * 2, b).astype(BF)
            pc_copy(r, k).start()
            return carry

        lax.fori_loop(0, 4, other, 0)

        def own(k, carry):
            part = wdot(core * 8 + hop(y, 1 + k) * 2, b)
            pc_copy(r, k).wait_recv()
            sum2[r, k] = (part + corerecv[r, k].astype(F32)).astype(BF)

            @pl.when(k < 3)
            def _():
                py_copy(r, k).start()

            return carry

        lax.fori_loop(0, 4, own, 0)

    def y_total(r, low):
        rows = pl.ds(mult(low * 128, 128), 128)
        return (
            (sum2[r, 3, rows, :].astype(F32) + yrecv[r, 0, rows, :].astype(F32))
            + (yrecv[r, 1, rows, :].astype(F32) + yrecv[r, 2, rows, :].astype(F32))
        )

    def stage_a(r):
        for k in range(3):
            py_copy(r, k).wait_recv()
        zlsend[r] = y_total(r, 1 - zl).astype(BF)
        pz_copy(r).start()

    def stage_b(r):
        pz_copy(r).wait_recv()
        xsend[r] = (y_total(r, zl) + zlrecv[r].astype(F32)).astype(BF)
        px_copy(r).start()

    def ddot(half, n):
        return lax.dot_general(
            cot[pl.ds(mult(half * 512, 512), 512), :],
            wb[pl.ds(n * 2, 2)].reshape(256, 3072),
            (((1,), (1,)), ((), ())),
            preferred_element_type=F32,
        )

    def dz_copy(n):
        return remote(dxsend.at[n], dxrecv.at[n], dz_s.at[n], dz_r.at[n], at(zh=1 - zh))

    def da_copy(n, i):
        to_x = hop(x, HOPS[i])
        return remote(
            dxown.at[n, pl.ds(mult(to_x * 128, 128), 128)],
            dxs_ref.at[x, :, pl.ds(mult(n * 256, 256), 256)],
            da_s.at[n, i], da_r.at[n, i], at(x=to_x),
        )

    def dl_copy(n):
        return pltpu.make_async_copy(
            dxown.at[n, pl.ds(mult(x * 128, 128), 128)],
            dxs_ref.at[x, :, pl.ds(mult(n * 256, 256), 256)],
            dl_s.at[n],
        )

    def d_other(n, carry):
        dxsend[n] = ddot(1 - zh, n).astype(BF)
        dz_copy(n).start()
        return carry

    def d_own(n, carry):
        part = ddot(zh, n)
        dz_copy(n).wait_recv()
        dxown[n] = (part + dxrecv[n].astype(F32)).astype(BF)
        for i in range(3):
            da_copy(n, i).start()
        dl_copy(n).start()
        return carry

    wgrad(0)
    c_copies[0].wait_recv()
    wgrad(1)
    c_copies[1].wait_recv()
    for i, half in ((2, 1 - zh), (3, zh)):
        part = cot_copy(i, half * 512, 512)
        copy = remote(part, part, c_s.at[i], c_r.at[i], at(x=hop(x, 2)))
        copy.start()
        c_copies.append(copy)
    wgrad(2)
    stage_a(0)
    for copy in wc_copies:
        copy.wait_recv()
    stage_a(1)
    stage_b(0)
    c_copies[2].wait_recv()
    lax.fori_loop(0, 4, d_other, 0)
    c_copies[3].wait_recv()
    wgrad(3)
    lax.fori_loop(4, 8, d_other, 0)
    stage_b(1)
    stage_a(2)
    lax.fori_loop(0, 4, d_own, 0)
    stage_b(2)
    stage_a(3)
    lax.fori_loop(4, 8, d_own, 0)
    stage_b(3)

    for copy in w_copies + wy_copies + wc_copies + x_copies + xz_copies + c_copies:
        copy.wait_send()
    px_copy(0).wait()
    for r in range(1, 4):
        px_copy(r).wait()

    for r in (2, 3):
        for k in range(4):
            pc_copy(r, k).wait_send()

    def drain_w(r, carry):
        for k in range(3):
            py_copy(r, k).wait_send()
        pz_copy(r).wait_send()
        return carry

    lax.fori_loop(0, 4, drain_w, 0)

    def drain_d(n, carry):
        dz_copy(n).wait_send()
        for i in range(3):
            da_copy(n, i).wait()
        dl_copy(n).wait()
        return carry

    lax.fori_loop(0, 8, drain_d, 0)


def core_call(layer_input, gain, wq, wk, wv, qg, kg, vg, pos, freq):
    vm = pl.BlockSpec(memory_space=pltpu.VMEM)
    hbm = pl.BlockSpec(memory_space=pl.ANY)
    dma = pltpu.SemaphoreType.DMA
    return pl.pallas_call(
        core_kernel,
        out_shape=(
            jax.ShapeDtypeStruct((4, 128, 2048), BF),
            jax.ShapeDtypeStruct((4, 128, 768), BF),
        ),
        in_specs=[vm, vm, hbm, hbm, hbm, vm, vm, vm, vm, vm],
        out_specs=(hbm, hbm),
        scratch_shapes=[
            pltpu.VMEM((4, 16, 128, 128), BF),
            pltpu.VMEM((16, 128, 1024), BF),
            pltpu.VMEM((1024, 3072), BF),
            pltpu.VMEM((16, 128, 3072), BF),
            pltpu.VMEM((2, 4, 256, 768), BF),
            pltpu.VMEM((4, 4, 256, 768), BF),
            pltpu.VMEM((4, 4, 256, 768), BF),
            pltpu.VMEM((4, 3, 256, 768), BF),
            pltpu.VMEM((4, 128, 768), BF),
            pltpu.VMEM((4, 128, 768), BF),
            pltpu.VMEM((4, 128, 768), BF),
            pltpu.VMEM((8, 512, 256), BF),
            pltpu.VMEM((8, 512, 256), BF),
            pltpu.VMEM((8, 512, 256), BF),
            dma((3, 3)), dma((3, 3)), dma((3,)),
            dma((3,)), dma((3,)), dma((4,)), dma((4,)),
            dma((3,)), dma((3,)), dma, dma((4,)), dma((4,)),
            dma((4,)), dma((4,)),
            dma((4, 4)), dma((4, 4)), dma((4, 3)), dma((4, 3)), dma((4,)), dma((4,)),
            dma((3,)), dma((3,)), dma,
            dma((8,)), dma((8,)), dma((8, 3)), dma((8, 3)), dma((8,)),
        ],
        compiler_params=pltpu.CompilerParams(
            collective_id=1, has_side_effects=True, vmem_limit_bytes=63 * 2**20
        ),
        cost_estimate=pl.CostEstimate(flops=26 * 10**9, bytes_accessed=20 * 10**6, transcendentals=0),
        name="projection_backward",
    )(layer_input, gain, wq, wk, wv, qg, kg, vg, pos, freq)


def norm_back_kernel(x_ref, gain_ref, d_ref, o_ref):
    rows = x_ref.shape[0]
    order = [(s, kappa) for s in range(4) for kappa in range(16)]

    def low(s, kappa):
        c, yy, zz = kappa // 8, (kappa // 2) % 4, kappa % 2
        return (yy * 4 + zz * 2 + c) * 512 + s * 128

    square = jnp.zeros((rows, 128), F32)
    cross = jnp.zeros((rows, 128), F32)
    for s, kappa in order:
        cols = pl.ds(low(s, kappa), 128)
        v = x_ref[:, cols].astype(F32)
        g = d_ref[s, :, pl.ds(kappa * 128, 128)].astype(F32) * gain_ref[:, cols]
        square = square + v * v
        cross = cross + v * g
    mean = jnp.sum(square, axis=1, keepdims=True) * (1.0 / 8192)
    rstd = lax.rsqrt(mean + 1e-05)
    dot = jnp.sum(cross, axis=1, keepdims=True) * (1.0 / 8192) * rstd
    for s, kappa in order:
        cols = pl.ds(low(s, kappa), 128)
        v = x_ref[:, cols].astype(F32)
        g = d_ref[s, :, pl.ds(kappa * 128, 128)].astype(F32) * gain_ref[:, cols]
        o_ref[:, cols] = (rstd * (g - (v * rstd) * dot)).astype(BF)


def norm_back(layer_input, gain, parts):
    rows = 32
    return pl.pallas_call(
        norm_back_kernel,
        out_shape=jax.ShapeDtypeStruct((128, 8192), BF),
        grid=(128 // rows,),
        in_specs=[
            pl.BlockSpec((rows, 8192), lambda i: (i, 0)),
            pl.BlockSpec((1, 8192), lambda i: (0, 0)),
            pl.BlockSpec((4, rows, 2048), lambda i: (0, i, 0)),
        ],
        out_specs=pl.BlockSpec((rows, 8192), lambda i: (i, 0)),
        compiler_params=pltpu.CompilerParams(vmem_limit_bytes=32 * 2**20),
        name="norm_backward",
    )(layer_input, gain, parts)


def shards(layer_input, norm_gain, wq, wk, wv, qg, kg, vg, positions):
    gain = norm_gain.reshape(1, 8192)
    index = (jnp.arange(HD, dtype=jnp.int32) % (HD // 2)).astype(F32)
    freq = jnp.exp(-(2.0 * index / HD) * jnp.log(10000.0)).reshape(1, HD)
    parts, sums = core_call(
        layer_input,
        gain,
        wq.reshape(4, 2, 2, 4, 128, 512),
        wk.reshape(4, 2, 2, 4, 128, 128),
        wv.reshape(4, 2, 2, 4, 128, 128),
        qg, kg, vg,
        positions.reshape(8, 128),
        freq,
    )
    input_grad = norm_back(layer_input, gain, parts)
    sums = sums.reshape(512, 768).astype(F32) * (1.0 / math.sqrt(16384))
    return input_grad, sums[:, 512:640], sums[:, 640:], sums[:, :512]


def solution(mesh):
    in_specs = (
        P(("dp", "mp"), None),
        P(),
        P(None, "mp"),
        P(None, "mp"),
        P(None, "mp"),
        P("dp", "mp"),
        P("dp", "mp"),
        P("dp", "mp"),
        P("dp"),
    )
    out_specs = (P(("dp", "mp"), None), P("dp", "mp"), P("dp", "mp"), P("dp", "mp"))
    return jax.shard_map(shards, mesh=mesh, in_specs=in_specs, out_specs=out_specs, check_vma=False)
```

time: 545 us -> 226 us (0.41)
  waiting for transfers between devices: 455 us -> 0 us
  Pallas kernels: 0 us -> 220 us
  matrix products: 48.5 us -> 0 us
  other arithmetic: 21.1 us -> 0.65 us
  between operations: 13.9 us -> 0.67 us
    reduce_scatter x2 -> x0, waiting for transfers between devices: 292 us -> none  [the longest x1 154 us: shards(): lax.psum_scatter(lax.dot_general(cotangent, weights, (((1,), (1,)), ((),...]
    pallas_call x0 -> x2, Pallas kernels: none -> 220 us  [the longest x1 216 us: core_call(): pl.pallas_call(core_kernel, out_shape=(jax.ShapeDtypeStruct((4, 128, 2048...]
    all_gather x1 -> x0, waiting for transfers between devices: 162 us -> none  [shards(): lax.all_gather(layer_input, 'mp', axis=0, tiled=True)]
    dot_general x2 -> x0, matrix products: 48.5 us -> none  [the longest x1 29.3 us: shards(): lax.dot_general(normed_piece, cotangent, (((0,), (0,)), ((), ())), prefer...]
    reduce_sum x3 -> x0, other arithmetic: 10.4 us -> none  [the longest x2 7.67 us: normalize(): jnp.mean(value_rows * value_rows, axis=-1, keepdims=True) + 1e-05]
  transfers between devices with their start and end apart: 3 -> 0, of which waited for: 3 -> 0; matrix products, arithmetic and copies ran while one was open for 13% -> 0% of each run, Pallas kernels for 0% -> 0%
where the time goes in v1:
time: 226 us
  Pallas kernels  220 us (97%)
  local copies, waits for them, and re-layouts  5.13 us (2%)
    pallas_call x1, Pallas kernels, core_call(): pl.pallas_call(core_kernel, out_shape=(jax.ShapeDtypeStruct((4, 128, 2048...  216 us

profile of v1, /device:TPU:1, one launch (start us, length us, event | category | flops | bytes accessed | tf_op | source)
XLA Modules:
  0.0 226.2 jit_solution(16138364966095393130)
XLA Ops:
  0.6 0.5 fusion.4.freq_ref
  1.2 0.0 copy-start.2
  1.2 216.4 %projection_backward.1 = (bf16[4,128,2048]{2,1,0:T(8,128)(2,1)}, bf16[4,128,768]{2,1,0:T(8,128)(2,1)}) custom-call(bf16[128,8192]{1,0:T(8,128)(2,1)} %x_ref.3, f32[1,8192]{1,0:T(1,128)} %bitcast.6, bf16[4,2,2,4,128,512]{5,4,3,2,1,0:T(8,128)(2,1)} %bitcast.10, bf16[4,2,2,4,128,128]{5,4,3,2,1,0:T(8,128)(2,1)} %bitcast.11, ...), custom_call_target="tpu_custom_call" | custom-call | flops 25999998976 | bytes 20000000 | tf_op jit(solution)/shard_map/projection_backward/pallas_call | solution.py:344
  217.5 0.0 copy-done.2
  217.5 0.0 copy-start
  217.6 1.6 copy-done
  219.1 0.0 copy-start.1
  219.1 1.6 copy-done.1
  220.7 0.0 copy-start.3
  220.7 3.4 %norm_backward.1 = bf16[128,8192]{1,0:T(8,128)(2,1)} custom-call(bf16[128,8192]{1,0:T(8,128)(2,1)S(1)} %copy-done, f32[1,8192]{1,0:T(1,128)S(1)} %bitcast.7, bf16[4,128,2048]{2,1,0:T(8,128)(2,1)S(1)} %copy-done.1), custom_call_target="tpu_custom_call" | custom-call | tf_op jit(solution)/shard_map/norm_backward/pallas_call | solution.py:411
  224.1 0.0 copy-done.3
  224.1 0.1 convert_multiply_fusion
  224.2 0.8 fusion.5
  225.1 1.1 slice.14
Async XLA Ops:
  1.2 216.4 %copy-start.2 = (f32[8192]{0:T(1024)S(1)}, f32[8192]{0:T(1024)}, u32[]{:S(2)}) copy-start(f32[8192]{0:T(1024)} %param.10) | copy-start | bytes 98308
  217.5 1.6 copy-start
  219.1 1.6 copy-start.1
  220.7 3.4 %copy-start.3 = (bf16[4,128,768]{2,1,0:T(8,128)(2,1)S(1)}, bf16[4,128,768]{2,1,0:T(8,128)(2,1)}, u32[]{:S(2)}) copy-start(bf16[4,128,768]{2,1,0:T(8,128)(2,1)} %get-tuple-element.7) | copy-start | bytes 2359300

commit v2 on v1

v2 whole, which is shorter than its diff:
```python
import functools
import math

import jax
import jax.numpy as jnp
import numpy as np
from jax import lax
from jax.experimental import pallas as pl
from jax.experimental.pallas import tpu as pltpu
from jax.sharding import PartitionSpec as P

HD = 128
NY, NX = 4, 4
HOPS = (1, 3, 2)
BF = jnp.bfloat16
F32 = jnp.float32
MESH = pl.DeviceIdType.MESH
FREQ = np.tile(10000.0 ** (-2.0 * np.arange(HD // 2) / HD), 2).astype(np.float32).reshape(1, HD)


def mult(value, by):
    return pl.multiple_of(value, by)


def core_kernel(
    x_ref, gain_ref, wq_ref, wk_ref, wv_ref, q_ref, k_ref, v_ref, pos_ref, freq_ref,
    dxs_ref, dws_ref,
    nt, xst, cot, wb, coresend, sum2, yrel, yrecv, zlsend, zlrecv, xsend, dxsend, dxrecv, dxown,
    w_s, w_r, wl_s, wy_s, wy_r, wq_s, wq_r, wc_s, wc_r, x_s, x_r, xl_s, xz_s, xz_r, c_s, c_r, cq_s, cq_r,
    pc_s, pc_r, ph_s, ph_r, py_s, py_r, pz_s, pz_r, px_s, px_r, pl_s, dz_s, dz_r, da_s, da_r, dl_s,
):
    dp = lax.axis_index("dp")
    mp = lax.axis_index("mp")
    y, zl, core = dp // 4, (dp // 2) % 2, dp % 2
    x, zh = mp // 2, mp % 2

    def at(y=y, zl=zl, core=core, x=x, zh=zh):
        return (y * 4 + zl * 2 + core, x * 2 + zh)

    def hop(v, k):
        return lax.rem(v + k, 4)

    def remote(src, dst, ssem, rsem, where):
        return pltpu.make_async_remote_copy(
            src_ref=src, dst_ref=dst, send_sem=ssem, recv_sem=rsem,
            device_id=where, device_id_type=MESH,
        )

    peers = [at(x=hop(x, k)) for k in HOPS] + [at(y=hop(y, k)) for k in (1, 3)]
    peers += [at(zl=1 - zl), at(zh=1 - zh), at(core=1 - core)]
    barrier = pltpu.get_barrier_semaphore()
    for peer in peers:
        pl.semaphore_signal(barrier, inc=1, device_id=peer, device_id_type=MESH)
    pl.semaphore_wait(barrier, len(peers))

    blocks = (x, hop(x, 3), hop(x, 1), hop(x, 2))
    own_rows = core * 8 + y * 2
    widths = ((wq_ref, 0, 512), (wk_ref, 512, 128), (wv_ref, 640, 128))

    def w_part(j, to_x):
        ref, low, width = widths[j]
        src = ref.at[y, :, core, to_x]
        dst = wb.at[pl.ds(own_rows, 2), :, pl.ds(mult(x * 768 + low, 128), width)]
        return src, dst

    def w_copy(i, j):
        to_x = hop(x, HOPS[i])
        src, dst = w_part(j, to_x)
        return remote(src, dst, w_s.at[i, j], w_r.at[i, j], at(x=to_x))

    def w_start(i):
        for j in range(3):
            w_copy(i, j).start()

    def w_wait(i):
        for j in range(3):
            w_copy(i, j).wait_recv()

    def w_rows(from_y, r):
        rows = pl.ds(core * 8 + from_y * 2, 2)
        if r is None:
            return wb.at[rows]
        return wb.at[rows, :, pl.ds(mult(blocks[r] * 768, 128), 768)]

    def wy_copy(r, s):
        part = w_rows(y, r)
        return remote(part, part, wy_s.at[r, s], wy_r.at[r, s], at(y=hop(y, (1, 3)[s])))

    def wq_copy(r):
        s = r // 2
        part = w_rows(hop(y, (3, 1)[s]), r)
        return remote(part, part, wq_s.at[r], wq_r.at[r], at(y=hop(y, (1, 3)[s])))

    def wc_copy(k):
        part = w_rows(hop(y, k), None)
        return remote(part, part, wc_s.at[k], wc_r.at[k], at(core=1 - core))

    def wy_start(r):
        wy_copy(r, 0).start()
        wy_copy(r, 1).start()

    w_local = []
    for j in range(3):
        src, dst = w_part(j, x)
        copy = pltpu.make_async_copy(src, dst, wl_s.at[j])
        copy.start()
        w_local.append(copy)
    w_start(0)
    w_start(1)
    for copy in w_local:
        copy.wait()
    wy_start(0)

    def squares(c, total):
        piece = x_ref[:, pl.ds(mult(c * 512, 512), 512)].astype(F32)
        piece = piece * piece
        return total + (piece[:, :128] + piece[:, 128:256]) + (piece[:, 256:384] + piece[:, 384:])

    total = lax.fori_loop(0, 16, squares, jnp.zeros((128, 128), F32))
    mean = jnp.sum(total, axis=1, keepdims=True) * (1.0 / 8192)
    rstd = lax.rsqrt(mean + 1e-05)

    def x_to(to_x):
        def block(kappa, carry):
            c, yy, zz = kappa // 8, (kappa // 2) % 4, kappa % 2
            low = mult((yy * 4 + zz * 2 + c) * 512 + to_x * 128, 128)
            rows = x_ref[:, pl.ds(low, 128)].astype(F32)
            normed = rows * rstd * gain_ref[:, pl.ds(low, 128)]
            nt[to_x, kappa] = normed.T.astype(BF)
            return carry

        lax.fori_loop(0, 16, block, 0)

    def x_slot(from_x):
        return xst.at[:, :, pl.ds(mult((zh * 4 + from_x) * 128, 128), 128)]

    def x_copy(i):
        to_x = hop(x, HOPS[i])
        return remote(nt.at[to_x], x_slot(x), x_s.at[i], x_r.at[i], at(x=to_x))

    def xz_copy(i):
        from_x = x if i == 3 else hop(x, 4 - HOPS[i])
        slot = x_slot(from_x)
        return remote(nt.at[x] if i == 3 else slot, slot, xz_s.at[i], xz_r.at[i], at(zh=1 - zh))

    x_to(x)
    x_local = pltpu.make_async_copy(nt.at[x], x_slot(x), xl_s)
    x_local.start()
    xz_copy(3).start()
    for i in (2, 0, 1):
        x_to(hop(x, HOPS[i]))
        x_copy(i).start()
    w_start(2)
    w_wait(0)
    wy_start(1)
    w_wait(1)
    wy_start(2)

    lane = lax.broadcasted_iota(jnp.int32, (128, 128), 1)

    def rope(t, carry):
        block = (t % 4) * 2 + t // 4
        rows = pl.ds(mult(block * 128, 128), 128)
        place = jnp.broadcast_to(pos_ref[pl.ds(block, 1), :].astype(F32), (128, 128)).T
        angle = place * freq_ref[...]
        cosine = jnp.cos(angle)
        sine = jnp.sin(angle)
        sine = jnp.where(lane < 64, sine, -sine)
        out = pl.ds(mult(t * 128, 128), 128)
        for h in range(5):
            v = q_ref[rows, pl.ds(h * 128, 128)] if h < 4 else k_ref[rows, :]
            v = v.astype(F32)
            back = v * cosine + pltpu.roll(v, 64, 1) * sine
            cot[out, pl.ds(mult(x * 768 + h * 128, 128), 128)] = back.astype(BF)
        cot[out, pl.ds(mult(x * 768 + 640, 128), 128)] = v_ref[rows, :]
        return carry

    lax.fori_loop(0, 8, rope, 0)

    def low_row(h):
        return (1 - zh if h == 0 else zh) * 512

    def c_copy(h, s):
        part = cot.at[pl.ds(mult(low_row(h), 512), 512), pl.ds(mult(x * 768, 128), 768)]
        return remote(part, part, c_s.at[h, s], c_r.at[h, s], at(x=hop(x, (1, 3)[s])))

    def cq_copy(h, s):
        b = blocks[1 + s]
        part = cot.at[pl.ds(mult(low_row(h) + s * 256, 256), 256), pl.ds(mult(b * 768, 128), 768)]
        return remote(part, part, cq_s.at[h, s], cq_r.at[h, s], at(x=hop(x, (1, 3)[s])))

    wy_copy(0, 0).wait_recv()
    wq_copy(0).start()
    for i in (0, 1):
        x_copy(i).wait_recv()
        xz_copy(i).start()
    c_copy(0, 0).start()
    c_copy(0, 1).start()
    wy_copy(1, 0).wait_recv()
    wq_copy(1).start()
    wy_copy(2, 1).wait_recv()
    wq_copy(2).start()
    x_copy(2).wait_recv()
    xz_copy(2).start()
    w_wait(2)
    wy_start(3)
    for s in (0, 1):
        c_copy(0, s).wait_recv()
        cq_copy(0, s).start()
    c_copy(1, 0).start()
    c_copy(1, 1).start()
    wy_copy(3, 1).wait_recv()
    wq_copy(3).start()
    wc_copy(0).start()
    for r in (0, 1, 2):
        wy_copy(r, 1 if r < 2 else 0).wait_recv()
    wy_copy(3, 0).wait_recv()
    wc_copy(3).start()
    wc_copy(1).start()
    for r in range(4):
        wq_copy(r).wait_recv()
    wc_copy(2).start()

    def wdot(kappa, b):
        return jnp.dot(
            xst[pl.ds(kappa, 2)].reshape(256, 1024),
            cot[:, pl.ds(mult(b * 768, 128), 768)],
            preferred_element_type=F32,
        )

    def chunk_y(k):
        return hop(y, 6 - k)

    def pc_copy(r, k):
        return remote(coresend.at[r % 2, k], sum2.at[r, k], pc_s.at[r, k], pc_r.at[r, k], at(core=1 - core))

    def ph_copy(r, s):
        src = sum2.at[r, 0, pl.ds(s * 128, 128)]
        return remote(src, yrel.at[r, s], ph_s.at[r, s], ph_r.at[r, s], at(y=hop(y, (1, 3)[s])))

    def py_copy(r, s):
        src = sum2.at[r, (1, 3)[s]]
        return remote(src, yrecv.at[r, s], py_s.at[r, s], py_r.at[r, s], at(y=hop(y, (1, 3)[s])))

    def pz_copy(r):
        return remote(zlsend.at[r], zlrecv.at[r], pz_s.at[r], pz_r.at[r], at(zl=1 - zl))

    def px_copy(r):
        if r == 0:
            return pltpu.make_async_copy(xsend.at[r], dws_ref.at[x], pl_s)
        return remote(xsend.at[r], dws_ref.at[x], px_s.at[r - 1], px_r.at[r - 1], at(x=blocks[r]))

    def wgrad(r):
        b = blocks[r]

        def other(k, carry):
            if r >= 2:
                pc_copy(r - 2, k).wait_send()
            coresend[r % 2, k] = wdot((1 - core) * 8 + chunk_y(k) * 2, b).astype(BF)
            pc_copy(r, k).start()
            return carry

        lax.fori_loop(0, 4, other, 0)

        def own(k, carry):
            part = wdot(core * 8 + chunk_y(k) * 2, b)
            pc_copy(r, k).wait_recv()
            sum2[r, k] = (part + sum2[r, k].astype(F32)).astype(BF)

            @pl.when(k == 0)
            def _():
                ph_copy(r, 0).start()
                ph_copy(r, 1).start()

            return carry

        lax.fori_loop(0, 4, own, 0)

    def wpass(r):
        for s in (0, 1):
            k = (1, 3)[s]
            rows = pl.ds(s * 128, 128)
            ph_copy(r, s).wait_recv()
            sum2[r, k, rows, :] = (sum2[r, k, rows, :].astype(F32) + yrel[r, s].astype(F32)).astype(BF)
            py_copy(r, s).start()

    def y_total(r, low):
        rows = pl.ds(mult(low * 128, 128), 128)
        return sum2[r, 2, rows, :].astype(F32) + (
            yrecv[r, 0, rows, :].astype(F32) + yrecv[r, 1, rows, :].astype(F32)
        )

    def stage_a(r):
        for s in (0, 1):
            py_copy(r, s).wait_recv()
        zlsend[r] = y_total(r, 1 - zl).astype(BF)
        pz_copy(r).start()

    def stage_b(r):
        pz_copy(r).wait_recv()
        xsend[r] = (y_total(r, zl) + zlrecv[r].astype(F32)).astype(BF)
        px_copy(r).start()

    def ddot(half, n):
        return lax.dot_general(
            cot[pl.ds(mult(half * 512, 512), 512), :],
            wb[pl.ds(n * 2, 2)].reshape(256, 3072),
            (((1,), (1,)), ((), ())),
            preferred_element_type=F32,
        )

    def dz_copy(n):
        return remote(dxsend.at[n], dxrecv.at[n], dz_s.at[n], dz_r.at[n], at(zh=1 - zh))

    def da_copy(n, i):
        to_x = hop(x, HOPS[i])
        return remote(
            dxown.at[n, pl.ds(mult(to_x * 128, 128), 128)],
            dxs_ref.at[x, :, pl.ds(mult(n * 256, 256), 256)],
            da_s.at[n, i], da_r.at[n, i], at(x=to_x),
        )

    def dl_copy(n):
        return pltpu.make_async_copy(
            dxown.at[n, pl.ds(mult(x * 128, 128), 128)],
            dxs_ref.at[x, :, pl.ds(mult(n * 256, 256), 256)],
            dl_s.at[n],
        )

    def d_other(n, carry):
        dxsend[n] = ddot(1 - zh, n).astype(BF)
        dz_copy(n).start()
        return carry

    def d_own(n, carry):
        part = ddot(zh, n)
        dz_copy(n).wait_recv()
        dxown[n] = (part + dxrecv[n].astype(F32)).astype(BF)
        for i in (2, 0, 1):
            da_copy(n, i).start()
        dl_copy(n).start()
        return carry

    x_local.wait()
    for i in (3, 0, 1, 2):
        xz_copy(i).wait_recv()
    wgrad(0)
    for s in (0, 1):
        cq_copy(0, s).wait_recv()
    for k in range(4):
        wc_copy(k).wait_recv()
    lax.fori_loop(0, 4, d_other, 0)
    wpass(0)
    lax.fori_loop(4, 8, d_other, 0)
    for s in (0, 1):
        c_copy(1, s).wait_recv()
        cq_copy(1, s).start()
    wgrad(1)
    wgrad(2)
    wpass(1)
    stage_a(0)
    for s in (0, 1):
        cq_copy(1, s).wait_recv()
    wpass(2)
    wgrad(3)
    stage_b(0)
    wpass(3)
    lax.fori_loop(0, 3, d_own, 0)
    stage_a(1)
    lax.fori_loop(3, 5, d_own, 0)
    stage_b(1)
    stage_a(2)
    lax.fori_loop(5, 7, d_own, 0)
    stage_b(2)
    stage_a(3)
    lax.fori_loop(7, 8, d_own, 0)
    stage_b(3)

    for i in range(3):
        for j in range(3):
            w_copy(i, j).wait_send()
        x_copy(i).wait_send()
    for r in range(4):
        wy_copy(r, 0).wait_send()
        wy_copy(r, 1).wait_send()
        wq_copy(r).wait_send()
        wc_copy(r).wait_send()
        xz_copy(r).wait_send()
    for h in (0, 1):
        for s in (0, 1):
            c_copy(h, s).wait_send()
            cq_copy(h, s).wait_send()
    for r in (2, 3):
        for k in range(4):
            pc_copy(r, k).wait_send()
    for r in range(4):
        for s in (0, 1):
            ph_copy(r, s).wait_send()
            py_copy(r, s).wait_send()
        pz_copy(r).wait_send()
        px_copy(r).wait()

    def drain(n, carry):
        dz_copy(n).wait_send()
        for i in range(3):
            da_copy(n, i).wait()
        dl_copy(n).wait()
        return carry

    lax.fori_loop(0, 8, drain, 0)


def core_call(layer_input, gain, wq, wk, wv, qg, kg, vg, pos, freq):
    vm = pl.BlockSpec(memory_space=pltpu.VMEM)
    hbm = pl.BlockSpec(memory_space=pl.ANY)
    dma = pltpu.SemaphoreType.DMA
    return pl.pallas_call(
        core_kernel,
        out_shape=(
            jax.ShapeDtypeStruct((4, 128, 2048), BF),
            jax.ShapeDtypeStruct((4, 128, 768), BF),
        ),
        in_specs=[vm, vm, hbm, hbm, hbm, vm, vm, vm, vm, vm],
        out_specs=(hbm, hbm),
        scratch_shapes=[
            pltpu.VMEM((4, 16, 128, 128), BF),
            pltpu.VMEM((16, 128, 1024), BF),
            pltpu.VMEM((1024, 3072), BF),
            pltpu.VMEM((16, 128, 3072), BF),
            pltpu.VMEM((2, 4, 256, 768), BF),
            pltpu.VMEM((4, 4, 256, 768), BF),
            pltpu.VMEM((4, 2, 128, 768), BF),
            pltpu.VMEM((4, 2, 256, 768), BF),
            pltpu.VMEM((4, 128, 768), BF),
            pltpu.VMEM((4, 128, 768), BF),
            pltpu.VMEM((4, 128, 768), BF),
            pltpu.VMEM((8, 512, 256), BF),
            pltpu.VMEM((8, 512, 256), BF),
            pltpu.VMEM((8, 512, 256), BF),
            dma((3, 3)), dma((3, 3)), dma((3,)),
            dma((4, 2)), dma((4, 2)), dma((4,)), dma((4,)), dma((4,)), dma((4,)),
            dma((3,)), dma((3,)), dma, dma((4,)), dma((4,)),
            dma((2, 2)), dma((2, 2)), dma((2, 2)), dma((2, 2)),
            dma((4, 4)), dma((4, 4)), dma((4, 2)), dma((4, 2)), dma((4, 2)), dma((4, 2)), dma((4,)), dma((4,)),
            dma((3,)), dma((3,)), dma,
            dma((8,)), dma((8,)), dma((8, 3)), dma((8, 3)), dma((8,)),
        ],
        compiler_params=pltpu.CompilerParams(
            collective_id=1, has_side_effects=True, vmem_limit_bytes=63 * 2**20
        ),
        cost_estimate=pl.CostEstimate(flops=26 * 10**9, bytes_accessed=20 * 10**6, transcendentals=0),
        name="projection_backward",
    )(layer_input, gain, wq, wk, wv, qg, kg, vg, pos, freq)


def norm_back_kernel(x_ref, gain_ref, d_ref, s_ref, o_ref, k_ref, v_ref, q_ref):
    rows = x_ref.shape[0]
    order = [(s, kappa) for s in range(4) for kappa in range(16)]
    factor = 1.0 / math.sqrt(16384)
    q_ref[...] = s_ref[0, :, :512].astype(F32) * factor
    k_ref[...] = s_ref[0, :, 512:640].astype(F32) * factor
    v_ref[...] = s_ref[0, :, 640:].astype(F32) * factor

    def low(s, kappa):
        c, yy, zz = kappa // 8, (kappa // 2) % 4, kappa % 2
        return (yy * 4 + zz * 2 + c) * 512 + s * 128

    square = jnp.zeros((rows, 128), F32)
    cross = jnp.zeros((rows, 128), F32)
    for s, kappa in order:
        cols = pl.ds(low(s, kappa), 128)
        v = x_ref[:, cols].astype(F32)
        g = d_ref[s, :, pl.ds(kappa * 128, 128)].astype(F32) * gain_ref[:, cols]
        square = square + v * v
        cross = cross + v * g
    mean = jnp.sum(square, axis=1, keepdims=True) * (1.0 / 8192)
    rstd = lax.rsqrt(mean + 1e-05)
    dot = jnp.sum(cross, axis=1, keepdims=True) * (1.0 / 8192) * rstd
    for s, kappa in order:
        cols = pl.ds(low(s, kappa), 128)
        v = x_ref[:, cols].astype(F32)
        g = d_ref[s, :, pl.ds(kappa * 128, 128)].astype(F32) * gain_ref[:, cols]
        o_ref[:, cols] = (rstd * (g - (v * rstd) * dot)).astype(BF)


def norm_back(layer_input, gain, parts, sums):
    rows = 32

    def out(width):
        return pl.BlockSpec((128, width), lambda i: (i, 0))

    return pl.pallas_call(
        norm_back_kernel,
        out_shape=(
            jax.ShapeDtypeStruct((128, 8192), BF),
            jax.ShapeDtypeStruct((512, 128), F32),
            jax.ShapeDtypeStruct((512, 128), F32),
            jax.ShapeDtypeStruct((512, 512), F32),
        ),
        grid=(128 // rows,),
        in_specs=[
            pl.BlockSpec((rows, 8192), lambda i: (i, 0)),
            pl.BlockSpec((1, 8192), lambda i: (0, 0)),
            pl.BlockSpec((4, rows, 2048), lambda i: (0, i, 0)),
            pl.BlockSpec((1, 128, 768), lambda i: (i, 0, 0)),
        ],
        out_specs=(pl.BlockSpec((rows, 8192), lambda i: (i, 0)), out(128), out(128), out(512)),
        compiler_params=pltpu.CompilerParams(vmem_limit_bytes=63 * 2**20),
        name="norm_backward",
    )(layer_input, gain, parts, sums)


def shards(layer_input, norm_gain, wq, wk, wv, qg, kg, vg, positions):
    gain = norm_gain.reshape(1, 8192)
    parts, sums = core_call(
        layer_input,
        gain,
        wq.reshape(4, 2, 2, 4, 128, 512),
        wk.reshape(4, 2, 2, 4, 128, 128),
        wv.reshape(4, 2, 2, 4, 128, 128),
        qg, kg, vg,
        positions.reshape(8, 128),
        jnp.asarray(FREQ),
    )
    return norm_back(layer_input, gain, parts, sums)


def solution(mesh):
    in_specs = (
        P(("dp", "mp"), None),
        P(),
        P(None, "mp"),
        P(None, "mp"),
        P(None, "mp"),
        P("dp", "mp"),
        P("dp", "mp"),
        P("dp", "mp"),
        P("dp"),
    )
    out_specs = (P(("dp", "mp"), None), P("dp", "mp"), P("dp", "mp"), P("dp", "mp"))
    return jax.shard_map(shards, mesh=mesh, in_specs=in_specs, out_specs=out_specs, check_vma=False)
```

time: 226 us -> 178 us (0.79)
  Pallas kernels: 220 us -> 177 us
  local copies, waits for them, and re-layouts: 5.13 us -> 0 us
    pallas_call x1, Pallas kernels: 216 us -> 172 us  [core_call(): pl.pallas_call(core_kernel, out_shape=(jax.ShapeDtypeStruct((4, 128, 2048...]
    unnamed x8 -> x0, local copies, waits for them, and re-layouts: 3.18 us -> none
where the time goes in v2:
time: 178 us
  Pallas kernels  177 us (99%)
    pallas_call x1, Pallas kernels, core_call(): pl.pallas_call(core_kernel, out_shape=(jax.ShapeDtypeStruct((4, 128, 2048...  172 us
    pallas_call x1, Pallas kernels, norm_back(): pl.pallas_call(norm_back_kernel, out_shape=(jax.ShapeDtypeStruct((128, 81...  5.58 us

profile of v2, /device:TPU:1, one launch (start us, length us, event | category | flops | bytes accessed | tf_op | source)
XLA Modules:
  0.0 177.9 jit_solution(4722347366199738684)
XLA Ops:
  0.6 171.7 %projection_backward.1 = (bf16[4,128,2048]{2,1,0:T(8,128)(2,1)}, bf16[4,128,768]{2,1,0:T(8,128)(2,1)}) custom-call(bf16[128,8192]{1,0:T(8,128)(2,1)} %x_ref.3, f32[1,8192]{1,0:T(1,128)} %bitcast.5, bf16[4,2,2,4,128,512]{5,4,3,2,1,0:T(8,128)(2,1)} %bitcast.7, bf16[4,2,2,4,128,128]{5,4,3,2,1,0:T(8,128)(2,1)} %bitcast.8, ...), custom_call_target="tpu_custom_call" | custom-call | flops 25999998976 | bytes 20000000 | tf_op jit(solution)/shard_map/projection_backward/pallas_call | solution.py:417
  172.3 5.6 %norm_backward.1 = (bf16[128,8192]{1,0:T(8,128)(2,1)}, f32[512,128]{1,0:T(8,128)}, f32[512,128]{1,0:T(8,128)}, f32[512,512]{1,0:T(8,128)}) custom-call(bf16[128,8192]{1,0:T(8,128)(2,1)} %x_ref.3, f32[1,8192]{1,0:T(1,128)} %bitcast.6, bf16[4,128,2048]{2,1,0:T(8,128)(2,1)} %get-tuple-element.6.d_ref, bf16[4,128,768]{2,1,0:T(8,128)(2,1)} %get-tuple-element.7.s_ref), custom_call_target="tpu_custom_call" | custom-call | tf_op jit(solution)/shard_map/norm_backward/pallas_call | solution.py:492

commit v3 on v2

--- a/solution.py
+++ b/solution.py
@@ -26,7 +26,7 @@
     x_ref, gain_ref, wq_ref, wk_ref, wv_ref, q_ref, k_ref, v_ref, pos_ref, freq_ref,
     dxs_ref, dws_ref,
     nt, xst, cot, wb, coresend, sum2, yrel, yrecv, zlsend, zlrecv, xsend, dxsend, dxrecv, dxown,
-    w_s, w_r, wl_s, wy_s, wy_r, wq_s, wq_r, wc_s, wc_r, x_s, x_r, xl_s, xz_s, xz_r, c_s, c_r, cq_s, cq_r,
+    w_s, w_r, wl_s, wz_s, wz_r, wy_s, wy_r, wq_s, wq_r, wc_s, wc_r, x_s, x_r, xl_s, xz_s, xz_r, c_s, c_r, cq_s, cq_r,
     pc_s, pc_r, ph_s, ph_r, py_s, py_r, pz_s, pz_r, px_s, px_r, pl_s, dz_s, dz_r, da_s, da_r, dl_s,
 ):
     dp = lax.axis_index("dp")
@@ -57,16 +57,15 @@
     own_rows = core * 8 + y * 2
     widths = ((wq_ref, 0, 512), (wk_ref, 512, 128), (wv_ref, 640, 128))
 
-    def w_part(j, to_x):
+    def w_copy(i, j):
         ref, low, width = widths[j]
-        src = ref.at[y, :, core, to_x]
-        dst = wb.at[pl.ds(own_rows, 2), :, pl.ds(mult(x * 768 + low, 128), width)]
-        return src, dst
-
-    def w_copy(i, j):
         to_x = hop(x, HOPS[i])
-        src, dst = w_part(j, to_x)
-        return remote(src, dst, w_s.at[i, j], w_r.at[i, j], at(x=to_x))
+        dst = wb.at[own_rows + zl, :, pl.ds(mult(x * 768 + low, 128), width)]
+        return remote(ref.at[y, zl, core, to_x], dst, w_s.at[i, j], w_r.at[i, j], at(x=to_x))
+
+    def wz_copy(r):
+        part = wb.at[own_rows + zl, :, pl.ds(mult(blocks[r] * 768, 128), 768)]
+        return remote(part, part, wz_s.at[r], wz_r.at[r], at(zl=1 - zl))
 
     def w_start(i):
         for j in range(3):
@@ -101,12 +100,15 @@
 
     w_local = []
     for j in range(3):
-        src, dst = w_part(j, x)
+        ref, low, width = widths[j]
+        src = ref.at[y, :, core, x]
+        dst = wb.at[pl.ds(own_rows, 2), :, pl.ds(mult(x * 768 + low, 128), width)]
         copy = pltpu.make_async_copy(src, dst, wl_s.at[j])
         copy.start()
         w_local.append(copy)
     w_start(0)
     w_start(1)
+    w_start(2)
     for copy in w_local:
         copy.wait()
     wy_start(0)
@@ -147,14 +149,15 @@
     x_local = pltpu.make_async_copy(nt.at[x], x_slot(x), xl_s)
     x_local.start()
     xz_copy(3).start()
-    for i in (2, 0, 1):
+    for i in range(3):
         x_to(hop(x, HOPS[i]))
         x_copy(i).start()
-    w_start(2)
-    w_wait(0)
-    wy_start(1)
-    w_wait(1)
-    wy_start(2)
+    for i in range(3):
+        w_wait(i)
+        wz_copy(i + 1).start()
+    for r in (1, 2):
+        wz_copy(r).wait_recv()
+        wy_start(r)
 
     lane = lax.broadcasted_iota(jnp.int32, (128, 128), 1)
 
@@ -194,24 +197,22 @@
     for i in (0, 1):
         x_copy(i).wait_recv()
         xz_copy(i).start()
-    c_copy(0, 0).start()
-    c_copy(0, 1).start()
+    wz_copy(3).wait_recv()
+    wy_start(3)
     wy_copy(1, 0).wait_recv()
     wq_copy(1).start()
     wy_copy(2, 1).wait_recv()
     wq_copy(2).start()
     x_copy(2).wait_recv()
     xz_copy(2).start()
-    w_wait(2)
-    wy_start(3)
+    c_copy(0, 0).start()
+    c_copy(0, 1).start()
+    wc_copy(0).start()
+    wy_copy(3, 1).wait_recv()
+    wq_copy(3).start()
     for s in (0, 1):
         c_copy(0, s).wait_recv()
         cq_copy(0, s).start()
-    c_copy(1, 0).start()
-    c_copy(1, 1).start()
-    wy_copy(3, 1).wait_recv()
-    wq_copy(3).start()
-    wc_copy(0).start()
     for r in (0, 1, 2):
         wy_copy(r, 1 if r < 2 else 0).wait_recv()
     wy_copy(3, 0).wait_recv()
@@ -220,6 +221,9 @@
     for r in range(4):
         wq_copy(r).wait_recv()
     wc_copy(2).start()
+    for s in (0, 1):
+        cq_copy(0, s).wait_send()
+        c_copy(1, s).start()
 
     def wdot(kappa, b):
         return jnp.dot(
@@ -250,7 +254,7 @@
             return pltpu.make_async_copy(xsend.at[r], dws_ref.at[x], pl_s)
         return remote(xsend.at[r], dws_ref.at[x], px_s.at[r - 1], px_r.at[r - 1], at(x=blocks[r]))
 
-    def wgrad(r):
+    def wother(r):
         b = blocks[r]
 
         def other(k, carry):
@@ -261,6 +265,9 @@
             return carry
 
         lax.fori_loop(0, 4, other, 0)
+
+    def wown(r):
+        b = blocks[r]
 
         def own(k, carry):
             part = wdot(core * 8 + chunk_y(k) * 2, b)
@@ -344,33 +351,38 @@
     x_local.wait()
     for i in (3, 0, 1, 2):
         xz_copy(i).wait_recv()
-    wgrad(0)
+    wother(0)
+    wown(0)
     for s in (0, 1):
         cq_copy(0, s).wait_recv()
     for k in range(4):
         wc_copy(k).wait_recv()
-    lax.fori_loop(0, 4, d_other, 0)
+    lax.fori_loop(0, 3, d_other, 0)
     wpass(0)
-    lax.fori_loop(4, 8, d_other, 0)
+    lax.fori_loop(3, 8, d_other, 0)
     for s in (0, 1):
         c_copy(1, s).wait_recv()
         cq_copy(1, s).start()
-    wgrad(1)
-    wgrad(2)
+    wother(1)
+    wown(1)
+    wother(2)
     wpass(1)
-    stage_a(0)
+    wown(2)
     for s in (0, 1):
         cq_copy(1, s).wait_recv()
+    wother(3)
     wpass(2)
-    wgrad(3)
+    wown(3)
+    lax.fori_loop(0, 2, d_own, 0)
+    wpass(3)
+    lax.fori_loop(2, 4, d_own, 0)
+    stage_a(0)
+    lax.fori_loop(4, 6, d_own, 0)
+    stage_a(1)
     stage_b(0)
-    wpass(3)
-    lax.fori_loop(0, 3, d_own, 0)
-    stage_a(1)
-    lax.fori_loop(3, 5, d_own, 0)
+    stage_a(2)
+    lax.fori_loop(6, 7, d_own, 0)
     stage_b(1)
-    stage_a(2)
-    lax.fori_loop(5, 7, d_own, 0)
     stage_b(2)
     stage_a(3)
     lax.fori_loop(7, 8, d_own, 0)
@@ -381,6 +393,8 @@
             w_copy(i, j).wait_send()
         x_copy(i).wait_send()
     for r in range(4):
+        if r > 0:
+            wz_copy(r).wait_send()
         wy_copy(r, 0).wait_send()
         wy_copy(r, 1).wait_send()
         wq_copy(r).wait_send()
@@ -389,7 +403,8 @@
     for h in (0, 1):
         for s in (0, 1):
             c_copy(h, s).wait_send()
-            cq_copy(h, s).wait_send()
+            if h == 1:
+                cq_copy(h, s).wait_send()
     for r in (2, 3):
         for k in range(4):
             pc_copy(r, k).wait_send()
@@ -437,7 +452,7 @@
             pltpu.VMEM((8, 512, 256), BF),
             pltpu.VMEM((8, 512, 256), BF),
             pltpu.VMEM((8, 512, 256), BF),
-            dma((3, 3)), dma((3, 3)), dma((3,)),
+            dma((3, 3)), dma((3, 3)), dma((3,)), dma((4,)), dma((4,)),
             dma((4, 2)), dma((4, 2)), dma((4,)), dma((4,)), dma((4,)), dma((4,)),
             dma((3,)), dma((3,)), dma, dma((4,)), dma((4,)),
             dma((2, 2)), dma((2, 2)), dma((2, 2)), dma((2, 2)),

time: 178 us -> 164 us (0.921)
  Pallas kernels: 177 us -> 162 us
    pallas_call x1, Pallas kernels: 172 us -> 156 us  [core_call(): pl.pallas_call(core_kernel, out_shape=(jax.ShapeDtypeStruct((4, 128, 2048...]
where the time goes in v3:
time: 164 us; the launch traced here: 162 us
  Pallas kernels  162 us (99%)
    pallas_call x1, Pallas kernels, core_call(): pl.pallas_call(core_kernel, out_shape=(jax.ShapeDtypeStruct((4, 128, 2048...  156 us
    pallas_call x1, Pallas kernels, norm_back(): pl.pallas_call(norm_back_kernel, out_shape=(jax.ShapeDtypeStruct((128, 81...  5.58 us

profile of v3, /device:TPU:1, one launch (start us, length us, event | category | flops | bytes accessed | tf_op | source)
XLA Modules:
  0.0 162.2 jit_solution(2323514611421056742)
XLA Ops:
  0.6 156.0 %projection_backward.1 = (bf16[4,128,2048]{2,1,0:T(8,128)(2,1)}, bf16[4,128,768]{2,1,0:T(8,128)(2,1)}) custom-call(bf16[128,8192]{1,0:T(8,128)(2,1)} %x_ref.3, f32[1,8192]{1,0:T(1,128)} %bitcast.5, bf16[4,2,2,4,128,512]{5,4,3,2,1,0:T(8,128)(2,1)} %bitcast.7, bf16[4,2,2,4,128,128]{5,4,3,2,1,0:T(8,128)(2,1)} %bitcast.8, ...), custom_call_target="tpu_custom_call" | custom-call | flops 25999998976 | bytes 20000000 | tf_op jit(solution)/shard_map/projection_backward/pallas_call | solution.py:432
  156.6 5.6 %norm_backward.1 = (bf16[128,8192]{1,0:T(8,128)(2,1)}, f32[512,128]{1,0:T(8,128)}, f32[512,128]{1,0:T(8,128)}, f32[512,512]{1,0:T(8,128)}) custom-call(bf16[128,8192]{1,0:T(8,128)(2,1)} %x_ref.3, f32[1,8192]{1,0:T(1,128)} %bitcast.6, bf16[4,128,2048]{2,1,0:T(8,128)(2,1)} %get-tuple-element.6.d_ref, bf16[4,128,768]{2,1,0:T(8,128)(2,1)} %get-tuple-element.7.s_ref), custom_call_target="tpu_custom_call" | custom-call | tf_op jit(solution)/shard_map/norm_backward/pallas_call | solution.py:507

commit v4 on v3

--- a/solution.py
+++ b/solution.py
@@ -118,7 +118,7 @@
         piece = piece * piece
         return total + (piece[:, :128] + piece[:, 128:256]) + (piece[:, 256:384] + piece[:, 384:])
 
-    total = lax.fori_loop(0, 16, squares, jnp.zeros((128, 128), F32))
+    total = lax.fori_loop(0, 16, squares, jnp.zeros((128, 128), F32), unroll=4)
     mean = jnp.sum(total, axis=1, keepdims=True) * (1.0 / 8192)
     rstd = lax.rsqrt(mean + 1e-05)
 
@@ -131,7 +131,7 @@
             nt[to_x, kappa] = normed.T.astype(BF)
             return carry
 
-        lax.fori_loop(0, 16, block, 0)
+        lax.fori_loop(0, 16, block, 0, unroll=4)
 
     def x_slot(from_x):
         return xst.at[:, :, pl.ds(mult((zh * 4 + from_x) * 128, 128), 128)]
@@ -178,7 +178,7 @@
         cot[out, pl.ds(mult(x * 768 + 640, 128), 128)] = v_ref[rows, :]
         return carry
 
-    lax.fori_loop(0, 8, rope, 0)
+    lax.fori_loop(0, 8, rope, 0, unroll=2)
 
     def low_row(h):
         return (1 - zh if h == 0 else zh) * 512

time: 164 us -> 163 us (level)
  Pallas kernels: 162 us -> 160 us
where the time goes in v4:
time: 163 us; the launch traced here: 161 us
  Pallas kernels  160 us (98%)
    pallas_call x1, Pallas kernels, core_call(): pl.pallas_call(core_kernel, out_shape=(jax.ShapeDtypeStruct((4, 128, 2048...  155 us
    pallas_call x1, Pallas kernels, norm_back(): pl.pallas_call(norm_back_kernel, out_shape=(jax.ShapeDtypeStruct((128, 81...  5.58 us

profile of v4, /device:TPU:1, one launch (start us, length us, event | category | flops | bytes accessed | tf_op | source)
XLA Modules:
  0.0 161.1 jit_solution(2155934879083573904)
XLA Ops:
  0.6 154.8 %projection_backward.1 = (bf16[4,128,2048]{2,1,0:T(8,128)(2,1)}, bf16[4,128,768]{2,1,0:T(8,128)(2,1)}) custom-call(bf16[128,8192]{1,0:T(8,128)(2,1)} %x_ref.3, f32[1,8192]{1,0:T(1,128)} %bitcast.5, bf16[4,2,2,4,128,512]{5,4,3,2,1,0:T(8,128)(2,1)} %bitcast.7, bf16[4,2,2,4,128,128]{5,4,3,2,1,0:T(8,128)(2,1)} %bitcast.8, ...), custom_call_target="tpu_custom_call" | custom-call | flops 25999998976 | bytes 20000000 | tf_op jit(solution)/shard_map/projection_backward/pallas_call | solution.py:432
  155.4 5.6 %norm_backward.1 = (bf16[128,8192]{1,0:T(8,128)(2,1)}, f32[512,128]{1,0:T(8,128)}, f32[512,128]{1,0:T(8,128)}, f32[512,512]{1,0:T(8,128)}) custom-call(bf16[128,8192]{1,0:T(8,128)(2,1)} %x_ref.3, f32[1,8192]{1,0:T(1,128)} %bitcast.6, bf16[4,128,2048]{2,1,0:T(8,128)(2,1)} %get-tuple-element.6.d_ref, bf16[4,128,768]{2,1,0:T(8,128)(2,1)} %get-tuple-element.7.s_ref), custom_call_target="tpu_custom_call" | custom-call | tf_op jit(solution)/shard_map/norm_backward/pallas_call | solution.py:507
